TPU v7x, 32 devices: a whole 2x2x4 slice. The times are simulated.
32 devices in a mesh: row: 8 (over z, x), col: 4 (over y, core).
Axes of the slice: x: 2, y: 2, z: 4, core: 2. Of those that a mesh axis runs over, the one named last changes fastest.
Arguments:
- deposit_maps: float32 [1024, 8192], P('row', 'col'), may hold values from -30 to 30, as said below
- test_matrix: float32 [8192, 256], P('col'), may hold values from -1 to 1
Outputs:
- scaled_basis: float32 [1024, 256], P('row')
- projected: float32 [256, 8192], P('row', 'col')
Inputs may be any that keep to these rules, and one draw needn't show every extreme that they name: `deposit_maps`: a dense real matrix.
All inputs are finite; a program needn't handle non-finite values.
Results may differ from a plain program's by a relative error of at most 0.0003.
Values sent between devices are 32-bit elements; how exact they have to be, the bound alone decides.
A program may use at most 64 MiB of HBM per device.

v0:
```python
import math

import jax
import jax.numpy as jnp
from jax import lax
from jax.sharding import PartitionSpec as P


def apply_factor(current, gram_matrix):
    lower_factor = jnp.linalg.cholesky(gram_matrix)
    identity = jnp.eye(gram_matrix.shape[0], dtype=jnp.float32)
    inverse = jax.scipy.linalg.solve_triangular(lower_factor, identity, lower=True)
    return jnp.dot(
        current, inverse.T, preferred_element_type=jnp.float32, precision=lax.Precision.HIGHEST
    )


def local_gram(current):
    return jnp.dot(
        current.T, current, preferred_element_type=jnp.float32, precision=lax.Precision.HIGHEST
    )


def passes_rows(current):
    for sweep_index in range(2):
        gram_matrix = lax.psum(local_gram(current), "row")
        current = apply_factor(current, gram_matrix)
    return current


def on_device(deposit_maps, test_matrix):
    partial_sketch = jnp.dot(
        deposit_maps,
        test_matrix,
        preferred_element_type=jnp.float32,
        precision=lax.Precision.HIGHEST,
    )
    sketch = lax.psum(partial_sketch, "col")
    orthonormal = passes_rows(sketch)
    total_rows = orthonormal.shape[0] * lax.axis_size("row")
    scaled_basis = orthonormal * math.sqrt(total_rows)
    projected = lax.psum_scatter(
        jnp.dot(
            orthonormal.T,
            deposit_maps,
            preferred_element_type=jnp.float32,
            precision=lax.Precision.HIGHEST,
        ),
        "row",
        scatter_dimension=0,
        tiled=True,
    )
    return (scaled_basis, projected)


def solution(mesh):
    placed = (P("row", "col"), P("col", None))
    return jax.shard_map(
        on_device,
        mesh=mesh,
        in_specs=placed,
        out_specs=(P("row", None), P("row", "col")),
        check_vma=False,
    )
```

profile of v0, /device:TPU:0, one launch (start us, length us, event | category | flops | bytes accessed | tf_op | source)
XLA Modules:
  0.0 415.3 jit_solution(9929776341706306491)
XLA Ops:
  7.2 1.5 copy-done
  8.8 3.0 fusion.29
  11.8 34.2 %all-reduce.5.cloned.1.call-done = f32[128,256]{1,0:T(8,128)} async-done(((f32[128,256]{1,0:T(8,128)}), f32[128,256]{1,0:T(8,128)}) %all-reduce.5.cloned.1.call-update) | async-done | bytes 131088 | tf_op jit(solution)/shard_map/psum | solution.py:38
  46.1 2.1 fusion.30
  48.3 72.6 %all-reduce.7.cloned.1.call-done = f32[256,256]{0,1:T(8,128)} async-done(((f32[256,256]{0,1:T(8,128)}), f32[256,256]{0,1:T(8,128)}) %all-reduce.7.cloned.1.call-update) | async-done | bytes 262160 | tf_op jit(solution)/shard_map/psum | solution.py:26
  120.9 1.1 copy.5
  123.0 11.7 %cholesky.130 = f32[128,128]{1,0:T(8,128)S(1)} custom-call(f32[128,128]{1,0:T(8,128)S(1)} %cholesky.194), custom_call_target="Cholesky" | custom-call | tf_op jit(solution)/shard_map/jit(cholesky)/cholesky | solution.py:10
  134.7 9.8 %custom-call.13 = f32[1,128,128]{1,2,0:T(8,128)S(1)} custom-call(f32[1,128,128]{2,1,0:T(8,128)S(1)} %get-tuple-element.47), custom_call_target="InvertDiagBlocksLowerTriangular" | custom-call | tf_op jit(solution)/shard_map/jit(cholesky)/cholesky | solution.py:10
  145.1 11.7 %cholesky.147 = f32[128,128]{1,0:T(8,128)S(1)} custom-call(f32[128,128]{1,0:T(8,128)S(1)} %convolution_subtract_fusion.3), custom_call_target="Cholesky" | custom-call | tf_op jit(solution)/shard_map/jit(cholesky)/cholesky | solution.py:10
  159.0 4.3 %while.4 = (s32[]{:T(128)}, f32[256,256]{1,0:T(8,128)S(1)}, s32[2,2]{1,0:T(2,128)S(1)}, f32[2,128,128]{2,1,0:T(8,128)S(1)}, s32[]{:T(128)}) while((s32[]{:T(128)}, f32[256,256]{1,0:T(8,128)S(1)}, s32[2,2]{1,0:T(2,128)S(1)}, f32[2,128,128]{2,1,0:T(8,128)S(1)}, s32[]{:T(128)}) %tuple.48), condition=%wide.while_cond, body=%wide.while_body.sunk | while | flops 2 | bytes 131189 | solution.py:12
  159.8 1.4 bitcast_dynamic-update-slice_fusion.4
  161.9 1.4 bitcast_dynamic-update-slice_fusion.4
  163.3 19.7 %custom-call.14 = f32[2,128,128]{1,2,0:T(8,128)S(1)} custom-call(f32[2,128,128]{2,1,0:T(8,128)S(1)} %get-tuple-element.18), custom_call_target="InvertDiagBlocksLowerTriangular" | custom-call | tf_op jit(solution)/shard_map/jit(_solve_triangular)/triangular_solve | solution.py:12
  184.3 1.1 fusion.31
  185.5 70.0 %all-reduce.9.cloned.1.call-done = f32[256,256]{0,1:T(8,128)} async-done(((f32[256,256]{0,1:T(8,128)}), f32[256,256]{0,1:T(8,128)}) %all-reduce.9.cloned.1.call-update) | async-done | bytes 262160 | tf_op jit(solution)/shard_map/psum | solution.py:26
  258.2 11.7 %cholesky.164 = f32[128,128]{1,0:T(8,128)S(1)} custom-call(f32[128,128]{1,0:T(8,128)S(1)} %cholesky.197), custom_call_target="Cholesky" | custom-call | tf_op jit(solution)/shard_map/jit(cholesky)/cholesky | solution.py:10
  270.7 10.4 %custom-call.15 = f32[1,128,128]{1,2,0:T(8,128)} custom-call(f32[1,128,128]{2,1,0:T(8,128)S(1)} %get-tuple-element.43), custom_call_target="InvertDiagBlocksLowerTriangular" | custom-call | tf_op jit(solution)/shard_map/jit(cholesky)/cholesky | solution.py:10
  281.1 1.6 cholesky.189
  282.8 1.7 constant_dynamic-update-slice_fusion.1
  284.5 1.7 convolution_subtract_fusion.2
  286.2 13.2 %cholesky.181 = f32[128,128]{1,0:T(8,128)} custom-call(f32[128,128]{1,0:T(8,128)} %convolution_subtract_fusion.2), custom_call_target="Cholesky" | custom-call | tf_op jit(solution)/shard_map/jit(cholesky)/cholesky | solution.py:10
  299.4 1.5 select_reduce_fusion
  302.9 1.7 select_select_fusion
  305.2 7.0 %while.5 = (s32[]{:T(128)}, f32[256,256]{1,0:T(8,128)}, s32[2,2]{1,0:T(2,128)S(1)}, f32[2,128,128]{2,1,0:T(8,128)}, s32[]{:T(128)}) while((s32[]{:T(128)}, f32[256,256]{1,0:T(8,128)}, s32[2,2]{1,0:T(2,128)S(1)}, f32[2,128,128]{2,1,0:T(8,128)}, s32[]{:T(128)}) %tuple.62), condition=%wide.while_cond.clone, body=%wide.while_body.clone.sunk | while | flops 2 | bytes 132205 | solution.py:12
  305.9 2.9 bitcast_dynamic-update-slice_fusion.5
  309.4 2.8 bitcast_dynamic-update-slice_fusion.5
  312.3 21.1 %custom-call.16 = f32[2,128,128]{1,2,0:T(8,128)} custom-call(f32[2,128,128]{2,1,0:T(8,128)} %get-tuple-element.19), custom_call_target="InvertDiagBlocksLowerTriangular" | custom-call | tf_op jit(solution)/shard_map/jit(_solve_triangular)/triangular_solve | solution.py:12
  333.3 1.1 fusion.11
  334.5 1.1 convolution_subtract_fusion
  335.6 1.1 fusion.16
  337.8 3.2 fusion.32
  341.1 67.7 %reduce-scatter.2.cloned.1.call-done = f32[32,2048]{1,0:T(8,128)} async-done(((f32[256,2048]{1,0:T(8,128)}), f32[32,2048]{1,0:T(8,128)}) %reduce-scatter.2.cloned.1.call-update) | async-done | bytes 262160 | tf_op jit(solution)/shard_map/reduce_scatter | solution.py:42
  (50 shorter events, 12.3 us)
Async XLA Ops:
  7.2 1.6 copy-start
  7.2 38.9 %all-reduce.5.cloned.1.call-start = ((), (), s32[]{:S(2)}) async-start(), calls=%async_computation.1 | async-start | bytes 262144 | tf_op jit(solution)/shard_map/psum | solution.py:38
  11.8 109.1 %all-reduce.7.cloned.1.call-start = ((), (), s32[]{:S(2)}) async-start(), calls=%async_computation.2 | async-start | bytes 524288 | tf_op jit(solution)/shard_map/psum | solution.py:26
  48.2 207.3 %all-reduce.9.cloned.1.call-start = ((), (), s32[]{:S(2)}) async-start(), calls=%async_computation.3 | async-start | bytes 524288 | tf_op jit(solution)/shard_map/psum | solution.py:26
  123.0 60.9 %copy-start.2 = (f32[128,256]{1,0:T(8,128)S(1)}, f32[128,256]{1,0:T(8,128)}, u32[]{:S(2)}) copy-start(f32[128,256]{1,0:T(8,128)} %all-reduce.5.cloned.1.call-done) | copy-start | bytes 393220
  185.4 223.3 %reduce-scatter.2.cloned.1.call-start = ((), (), s32[]{:S(2)}) async-start(), calls=%async_computation.4 | async-start | bytes 2359296 | tf_op jit(solution)/shard_map/reduce_scatter | solution.py:42
  257.5 0.7 copy-start.3
  269.9 0.8 copy-start.4
  281.1 56.7 %copy-start.1 = (f32[128,2048]{1,0:T(8,128)S(1)}, f32[128,2048]{1,0:T(8,128)}, u32[]{:S(2)}) copy-start(f32[128,2048]{1,0:T(8,128)} %param.5) | copy-start | bytes 3145732
Sparse Core Ops, SparseCore 0:
  11.9 34.0 all-reduce.4
  50.3 70.5 all-reduce.6
  185.6 69.8 all-reduce.8
  341.2 67.5 reduce-scatter.1
where the time goes:
time: 416 us; the launch traced here: 415 us
  waiting for transfers between devices  245 us (59%)
  other arithmetic  117 us (28%)
  matrix products  19.1 us (5%)
  local copies, waits for them, and re-layouts  17.9 us (4%)
  between operations  16.6 us (4%)
    psum x2, waiting for transfers between devices, passes_rows(): gram_matrix = lax.psum(local_gram(current), 'row')  143 us
    another operation x13, other arithmetic, apply_factor(): lower_factor = jnp.linalg.cholesky(gram_matrix)  72.2 us
    reduce_scatter x1, waiting for transfers between devices, on_device(): lax.psum_scatter(jnp.dot(orthonormal.T, deposit_maps, preferred_element_t...  67.7 us
    another operation x5, other arithmetic, apply_factor(): jax.scipy.linalg.solve_triangular(lower_factor, identity, lower=True)  42.5 us
    psum x1, waiting for transfers between devices, on_device(): sketch = lax.psum(partial_sketch, 'col')  34.2 us
    another operation x15, local copies, waits for them, and re-layouts, apply_factor(): jax.scipy.linalg.solve_triangular(lower_factor, identity, lower=True)  11.8 us
  transfers between devices with their start and end apart: 4, of which 4 were waited for; matrix products, arithmetic and copies ran while one was open for 0% of the time, Pallas kernels for 0%

commit v1 on v0

v1 whole, which is shorter than its diff:
```python
import functools
import math

import jax
import jax.numpy as jnp
from jax import lax
from jax.experimental import pallas as pl
from jax.experimental.pallas import tpu as pltpu
from jax.sharding import PartitionSpec as P

MESH = pl.DeviceIdType.MESH
VMEM = pl.BlockSpec(memory_space=pltpu.VMEM)
BLOCK = 32


def dot(left, right, contract):
    return lax.dot_general(
        left,
        right,
        ((contract[:1], contract[1:]), ((), ())),
        preferred_element_type=jnp.float32,
        precision=lax.Precision.HIGHEST,
    )


def small_inverse(block):
    b = block.shape[0]
    row_index = lax.broadcasted_iota(jnp.int32, (b, 128), 0)
    lane = lax.broadcasted_iota(jnp.int32, (b, 128), 1)
    work = jnp.where(lane < b, block, jnp.where(lane == row_index + b, 1.0, 0.0))
    scale = jnp.zeros((b, 128), jnp.float32)
    for k in range(b):
        column = jnp.broadcast_to(work[:, k : k + 1], (b, 128))
        row = jnp.broadcast_to(work[k : k + 1, :], (b, 128))
        pivot = jnp.broadcast_to(column[k : k + 1, :], (b, 128))
        scale = jnp.where(row_index == k, pivot, scale)
        work = jnp.where(row_index > k, work - (column / pivot) * row, work)
    work = work * lax.rsqrt(scale)
    return work[:, b : 2 * b]


def factor_inverse(x_ref):
    size = x_ref.shape[0]
    lane = lax.broadcasted_iota(jnp.int32, (BLOCK, size), 1)
    row_index = lax.broadcasted_iota(jnp.int32, (BLOCK, size), 0)
    all_rows = lax.broadcasted_iota(jnp.int32, (size, size), 0)
    all_lanes = lax.broadcasted_iota(jnp.int32, (size, size), 1)

    def step(i, carry):
        start = pl.multiple_of(i * BLOCK, BLOCK)
        rows = x_ref[pl.ds(start, BLOCK), :]
        diagonal = pltpu.roll(rows, lax.rem(size - start, size), 1)[:, :128]
        inverse = small_inverse(diagonal)
        inside = (lane >= start) & (lane < start + BLOCK)
        rows = jnp.where(inside, jnp.where(lane == start + row_index, 1.0, 0.0), rows)
        done = dot(inverse, rows, (1, 0))
        upper = jnp.where(lane >= start + BLOCK, done, 0.0)
        update = dot(upper, done, (0, 0))
        below = all_rows >= start + BLOCK
        cleared = (all_lanes >= start) & (all_lanes < start + BLOCK)
        x_ref[...] = jnp.where(below & cleared, 0.0, x_ref[...]) - update
        x_ref[pl.ds(start, BLOCK), :] = done
        return carry

    lax.fori_loop(0, size // BLOCK, step, 0)
    x_ref[...] = jnp.where(all_lanes <= all_rows, x_ref[...], 0.0)


def first_pass_kernel(
    dims, maps_ref, test_ref, basis_ref, gram_ref, proj_ref,
    part, landed, sketch, columns, factor,
    col_send, col_recv, z_send, z_recv, xy_send, xy_recv, core_send, core_recv, a_send, a_recv,
):
    n_row, n_col, n_z = dims
    r, c = lax.axis_index("row"), lax.axis_index("col")
    z, x = r // 2, lax.rem(r, 2)
    y, core = c // 2, lax.rem(c, 2)
    width = columns.shape[-1]
    size = factor.shape[0]

    def device(z_to, x_to, y_to, core_to):
        return (z_to * 2 + x_to, y_to * 2 + core_to)

    barrier = pltpu.get_barrier_semaphore()
    for k in range(1, n_row):
        pl.semaphore_signal(
            barrier, inc=1, device_id=(lax.rem(r + k, n_row), c), device_id_type=MESH
        )
    for k in range(1, n_col):
        pl.semaphore_signal(
            barrier, inc=1, device_id=(r, lax.rem(c + k, n_col)), device_id_type=MESH
        )

    sub = part.shape[1]
    depth = maps_ref.shape[-1]
    own_maps = maps_ref[...].reshape(n_col * sub, depth)
    part[...] = dot(own_maps, test_ref[...], (1, 0)).reshape(part.shape)
    pl.semaphore_wait(barrier, n_row - 1 + n_col - 1)

    def send(source, target, send_sem, recv_sem, to):
        copy = pltpu.make_async_remote_copy(
            src_ref=source, dst_ref=target, send_sem=send_sem, recv_sem=recv_sem,
            device_id=to, device_id_type=MESH,
        )
        copy.start()
        return copy

    copies = []
    for k in range(1, n_col):
        to = lax.rem(c + k, n_col)
        copies.append(
            send(part.at[to], landed.at[k - 1], col_send.at[k - 1], col_recv.at[k - 1], (r, to))
        )
    total = part[c]
    for k, copy in enumerate(copies):
        copy.wait_recv()
        total = total + landed[k]
    sketch[y, core, x, z] = total
    sent = list(copies)

    copies = []
    for k in range(1, n_z):
        mine = sketch.at[y, core, x, z]
        to = device(lax.rem(z + k, n_z), x, y, core)
        copies.append(send(mine, mine, z_send.at[k - 1], z_recv.at[k - 1], to))
    for copy in copies:
        copy.wait_recv()
    sent += copies

    x_peer, y_peer = device(z, 1 - x, y, core), device(z, x, 1 - y, core)
    half = n_z // 2
    low, high = pl.ds(0, half), pl.ds(half, half)
    a = sketch.at[y, core, x, low]
    b = sketch.at[y, core, x, high]
    copies = [
        send(a, a, xy_send.at[0], xy_recv.at[0], x_peer),
        send(b, b, xy_send.at[1], xy_recv.at[1], y_peer),
    ]
    for copy in copies:
        copy.wait_recv()
    sent += copies
    a = sketch.at[y, core, :, low]
    b = sketch.at[:, core, x, high]
    copies = [
        send(a, a, xy_send.at[2], xy_recv.at[2], y_peer),
        send(b, b, xy_send.at[3], xy_recv.at[3], x_peer),
    ]
    for copy in copies:
        copy.wait_recv()
    sent += copies

    mine = sketch.at[:, core]
    core_copy = send(mine, mine, core_send, core_recv, device(z, x, y, 1 - core))
    core_copy.wait_recv()
    sent.append(core_copy)

    a_copies = []
    for k in range(1, n_row):
        to = lax.rem(r + k, n_row)
        share = pl.ds(pl.multiple_of(to * width, width), width)
        a_copies.append(
            send(
                maps_ref.at[:, :, :, share], columns.at[:, :, x, z],
                a_send.at[k - 1], a_recv.at[k - 1], (to, c),
            )
        )
    share = pl.ds(pl.multiple_of(r * width, width), width)
    columns[:, :, x, z] = maps_ref[:, :, :, share]

    chunks = [(i, j) for i in range(n_col // 2) for j in range(2)]
    gram = None
    for i, j in chunks:
        rows = sketch[i, j].reshape(-1, size)
        term = dot(rows, rows, (0, 0))
        gram = term if gram is None else gram + term
    factor[...] = gram
    factor_inverse(factor)
    inverse = factor[...]
    for copy in sent:
        copy.wait_send()
    gram = None
    for i, j in chunks:
        rows = dot(sketch[i, j].reshape(-1, size), inverse, (1, 1))
        sketch[i, j] = rows.reshape(sketch.shape[2:])
        term = dot(rows, rows, (0, 0))
        gram = term if gram is None else gram + term
    gram_ref[...] = gram
    basis_ref[...] = sketch[:, :, x, z]
    for copy in a_copies:
        copy.wait()
    proj = None
    for i, j in chunks:
        term = dot(
            sketch[i, j].reshape(-1, size), columns[i, j].reshape(-1, width), (0, 0)
        )
        proj = term if proj is None else proj + term
    proj_ref[...] = proj


def second_pass_kernel(total_rows, gram_ref, basis_ref, proj_ref, scaled_ref, out_ref, factor):
    size = gram_ref.shape[0]
    row_index = lax.broadcasted_iota(jnp.int32, (size, size), 0)
    lane = lax.broadcasted_iota(jnp.int32, (size, size), 1)
    identity = jnp.where(row_index == lane, 1.0, 0.0)
    weight = jnp.where(lane < row_index, 1.0, 0.5 * identity)
    gram = gram_ref[...]
    error = gram - identity
    small = jnp.sum(error * error) <= 4e-4

    @pl.when(small)
    def _():
        inverse = identity - weight * error
        left = error - dot(weight * error, gram, (1, 0))
        residual = left - dot(identity + left, weight * error, (1, 1))
        factor[...] = inverse - dot(weight * residual, inverse, (1, 0))

    @pl.when(jnp.logical_not(small))
    def _():
        factor[...] = gram
        factor_inverse(factor)

    inverse = factor[...]
    scaled_ref[...] = dot(basis_ref[...], inverse, (1, 1)) * math.sqrt(total_rows)
    out_ref[...] = dot(inverse, proj_ref[...], (1, 0))


def spread_kernel(n_row, proj_ref, out_ref, send_sem, recv_sem):
    r, c = lax.axis_index("row"), lax.axis_index("col")
    width = proj_ref.shape[-1]
    barrier = pltpu.get_barrier_semaphore()
    for k in range(1, n_row):
        pl.semaphore_signal(
            barrier, inc=1, device_id=(lax.rem(r + k, n_row), c), device_id_type=MESH
        )
    share = pl.ds(pl.multiple_of(r * width, width), width)
    out_ref[:, share] = proj_ref[r]
    pl.semaphore_wait(barrier, n_row - 1)
    copies = []
    for k in range(1, n_row):
        to = lax.rem(r + k, n_row)
        copy = pltpu.make_async_remote_copy(
            src_ref=proj_ref.at[to], dst_ref=out_ref.at[:, share],
            send_sem=send_sem.at[k - 1], recv_sem=recv_sem.at[k - 1],
            device_id=(to, c), device_id_type=MESH,
        )
        copy.start()
        copies.append(copy)
    for copy in copies:
        copy.wait()


def gathered(deposit_maps, test_matrix):
    n_row, n_col = lax.axis_size("row"), lax.axis_size("col")
    rows, depth = deposit_maps.shape
    size = test_matrix.shape[1]
    sub, width, n_z = rows // n_col, depth // n_row, n_row // 2
    f32 = jnp.float32
    maps = deposit_maps.reshape(n_col // 2, 2, sub, depth)
    dma = pltpu.SemaphoreType.DMA
    basis, gram, proj = pl.pallas_call(
        functools.partial(first_pass_kernel, (n_row, n_col, n_z)),
        out_shape=(
            jax.ShapeDtypeStruct((n_col // 2, 2, sub, size), f32),
            jax.ShapeDtypeStruct((size, size), f32),
            jax.ShapeDtypeStruct((size, width), f32),
        ),
        in_specs=[VMEM, VMEM],
        out_specs=(VMEM, VMEM, VMEM),
        scratch_shapes=[
            pltpu.VMEM((n_col, sub, size), f32),
            pltpu.VMEM((n_col - 1, sub, size), f32),
            pltpu.VMEM((n_col // 2, 2, 2, n_z, sub, size), f32),
            pltpu.VMEM((n_col // 2, 2, 2, n_z, sub, width), f32),
            pltpu.VMEM((size, size), f32),
            dma((n_col - 1,)), dma((n_col - 1,)),
            dma((n_z - 1,)), dma((n_z - 1,)),
            dma((4,)), dma((4,)),
            dma, dma,
            dma((n_row - 1,)), dma((n_row - 1,)),
        ],
        compiler_params=pltpu.CompilerParams(
            collective_id=0, has_side_effects=True, vmem_limit_bytes=40 * 2**20
        ),
    )(maps, test_matrix)
    scaled, full = pl.pallas_call(
        functools.partial(second_pass_kernel, rows * n_row),
        out_shape=(
            jax.ShapeDtypeStruct((rows, size), f32),
            jax.ShapeDtypeStruct((size, width), f32),
        ),
        in_specs=[VMEM, VMEM, VMEM],
        out_specs=(VMEM, VMEM),
        scratch_shapes=[pltpu.VMEM((size, size), f32)],
        compiler_params=pltpu.CompilerParams(vmem_limit_bytes=32 * 2**20),
    )(gram, basis.reshape(rows, size), proj)
    projected = pl.pallas_call(
        functools.partial(spread_kernel, n_row),
        out_shape=jax.ShapeDtypeStruct((size // n_row, depth), f32),
        in_specs=[VMEM],
        out_specs=VMEM,
        scratch_shapes=[dma((n_row - 1,)), dma((n_row - 1,))],
        compiler_params=pltpu.CompilerParams(
            collective_id=1, has_side_effects=True, vmem_limit_bytes=32 * 2**20
        ),
    )(full.reshape(n_row, size // n_row, width))
    return scaled, projected


def apply_factor(current, gram_matrix):
    lower_factor = jnp.linalg.cholesky(gram_matrix)
    identity = jnp.eye(gram_matrix.shape[0], dtype=jnp.float32)
    inverse = jax.scipy.linalg.solve_triangular(lower_factor, identity, lower=True)
    return dot(current, inverse, (1, 1))


def summed(deposit_maps, test_matrix):
    current = lax.psum(dot(deposit_maps, test_matrix, (1, 0)), "col")
    for _ in range(2):
        gram_matrix = lax.psum(dot(current, current, (0, 0)), "row")
        current = apply_factor(current, gram_matrix)
    total_rows = current.shape[0] * lax.axis_size("row")
    projected = lax.psum_scatter(
        dot(current, deposit_maps, (0, 0)), "row", scatter_dimension=0, tiled=True
    )
    return current * math.sqrt(total_rows), projected


def on_device(deposit_maps, test_matrix):
    n_row, n_col = lax.axis_size("row"), lax.axis_size("col")
    rows, depth = deposit_maps.shape
    size = test_matrix.shape[1]
    fits = (
        n_col == 4
        and n_row % 4 == 0
        and rows % (n_col * 16) == 0
        and depth % (n_row * 128) == 0
        and size % (n_row * 8) == 0
        and size % 128 == 0
        and rows * n_row * size * 4 <= 4 * 2**20
        and depth * rows * 4 <= 4 * 2**20
        and depth * size * 4 <= 4 * 2**20
    )
    if fits:
        return gathered(deposit_maps, test_matrix)
    return summed(deposit_maps, test_matrix)


def solution(mesh):
    placed = (P("row", "col"), P("col", None))
    return jax.shard_map(
        on_device,
        mesh=mesh,
        in_specs=placed,
        out_specs=(P("row", None), P("row", "col")),
        check_vma=False,
    )
```

time: 416 us -> 82.4 us (0.20)
  waiting for transfers between devices: 245 us -> 0 us
  other arithmetic: 117 us -> 0 us
  Pallas kernels: 0 us -> 77 us
  matrix products: 19.1 us -> 0 us
  between operations: 16.6 us -> 0.66 us
  local copies, waits for them, and re-layouts: 17.9 us -> 3.51 us
    psum x3 -> x0, waiting for transfers between devices: 177 us -> none  [the longest x2 143 us: passes_rows(): gram_matrix = lax.psum(local_gram(current), 'row')]
    another operation x18 -> x0, other arithmetic: 115 us -> none  [the longest x13 72.2 us: apply_factor(): lower_factor = jnp.linalg.cholesky(gram_matrix)]
    pallas_call x0 -> x3, Pallas kernels: none -> 77 us  [the longest x1 66 us: gathered(): pl.pallas_call(functools.partial(first_pass_kernel, (n_row, n_col, n_z)),...]
    reduce_scatter x1 -> x0, waiting for transfers between devices: 67.7 us -> none  [on_device(): lax.psum_scatter(jnp.dot(orthonormal.T, deposit_maps, preferred_element_t...]
    another operation x19 -> x0, local copies, waits for them, and re-layouts: 13.5 us -> none  [the longest x15 11.8 us: apply_factor(): jax.scipy.linalg.solve_triangular(lower_factor, identity, lower=True)]
    dot_general x6 -> x0, matrix products: 10.9 us -> none  [the longest x2 3.21 us: local_gram(): jnp.dot(current.T, current, preferred_element_type=jnp.float32, precision...]
    another operation x10 -> x0, matrix products: 8.2 us -> none  [the longest x6 4.29 us: apply_factor(): jax.scipy.linalg.solve_triangular(lower_factor, identity, lower=True)]
  transfers between devices with their start and end apart: 4 -> 0, of which waited for: 4 -> 0; matrix products, arithmetic and copies ran while one was open for 0% -> 0% of each run, Pallas kernels for 0% -> 0%
where the time goes in v1:
time: 82.4 us; the launch traced here: 81.2 us
  Pallas kernels  77 us (93%)
  local copies, waits for them, and re-layouts  3.51 us (4%)
    pallas_call x1, Pallas kernels, gathered(): pl.pallas_call(functools.partial(first_pass_kernel, (n_row, n_col, n_z)),...  66 us
    pallas_call x1, Pallas kernels, gathered(): pl.pallas_call(functools.partial(spread_kernel, n_row), out_shape=jax.Sha...  8.27 us
    unnamed x5, local copies, waits for them, and re-layouts  3.51 us
    pallas_call x1, Pallas kernels, gathered(): pl.pallas_call(functools.partial(second_pass_kernel, rows * n_row), out_s...  2.76 us

profile of v1, /device:TPU:0, one launch (start us, length us, event | category | flops | bytes accessed | tf_op | source)
XLA Modules:
  0.0 81.2 jit_solution(66607740767714961)
XLA Ops:
  0.6 0.0 copy-start
  0.6 1.6 %copy-done = f32[2048,256]{1,0:T(8,128)S(1)} copy-done((f32[2048,256]{1,0:T(8,128)S(1)}, f32[2048,256]{1,0:T(8,128)}, u32[]{:S(2)}) %copy-start) | copy-done | bytes 2097176
  2.2 0.0 copy-start.1
  2.2 1.2 %copy-done.1 = f32[128,2048]{1,0:T(8,128)S(1)} copy-done((f32[128,2048]{1,0:T(8,128)S(1)}, f32[128,2048]{1,0:T(8,128)}, u32[]{:S(2)}) %copy-start.1) | copy-done | bytes 1048600
  3.4 66.0 %shard_map.41 = (f32[2,2,32,256]{3,2,1,0:T(8,128)S(1)}, f32[256,256]{1,0:T(8,128)S(1)}, f32[256,256]{1,0:T(8,128)S(1)}) custom-call(f32[2,2,32,2048]{3,2,1,0:T(8,128)S(1)} %bitcast.3, f32[2048,256]{1,0:T(8,128)S(1)} %copy-done), custom_call_target="tpu_custom_call" | custom-call | tf_op jit(solution)/shard_map/pallas_call | solution.py:260
  69.4 2.8 %shard_map.42 = (f32[128,256]{1,0:T(8,128)}, f32[256,256]{1,0:T(8,128)S(1)}) custom-call(f32[256,256]{1,0:T(8,128)S(1)} %get-tuple-element.7.gram_ref, f32[128,256]{1,0:T(8,128)S(1)} %bitcast.5, f32[256,256]{1,0:T(8,128)S(1)} %get-tuple-element.9.proj_ref), custom_call_target="tpu_custom_call" | custom-call | tf_op jit(solution)/shard_map/pallas_call | solution.py:285
  72.2 8.3 %shard_map.43 = f32[32,2048]{1,0:T(8,128)S(1)} custom-call(f32[8,32,256]{2,1,0:T(8,128)S(1)} %bitcast.4), custom_call_target="tpu_custom_call" | custom-call | tf_op jit(solution)/shard_map/pallas_call | solution.py:296
  80.5 0.7 copy.5
Async XLA Ops:
  0.6 1.6 %copy-start = (f32[2048,256]{1,0:T(8,128)S(1)}, f32[2048,256]{1,0:T(8,128)}, u32[]{:S(2)}) copy-start(f32[2048,256]{1,0:T(8,128)} %test_ref.1) | copy-start | bytes 6291460
  2.2 1.2 %copy-start.1 = (f32[128,2048]{1,0:T(8,128)S(1)}, f32[128,2048]{1,0:T(8,128)}, u32[]{:S(2)}) copy-start(f32[128,2048]{1,0:T(8,128)} %param.2) | copy-start | bytes 3145732

commit v2 on v1

--- a/solution.py
+++ b/solution.py
@@ -10,7 +10,8 @@
 
 MESH = pl.DeviceIdType.MESH
 VMEM = pl.BlockSpec(memory_space=pltpu.VMEM)
-BLOCK = 32
+BLOCK = 64
+PIECES = 4
 
 
 def dot(left, right, contract):
@@ -28,15 +29,42 @@
     row_index = lax.broadcasted_iota(jnp.int32, (b, 128), 0)
     lane = lax.broadcasted_iota(jnp.int32, (b, 128), 1)
     work = jnp.where(lane < b, block, jnp.where(lane == row_index + b, 1.0, 0.0))
-    scale = jnp.zeros((b, 128), jnp.float32)
-    for k in range(b):
-        column = jnp.broadcast_to(work[:, k : k + 1], (b, 128))
-        row = jnp.broadcast_to(work[k : k + 1, :], (b, 128))
-        pivot = jnp.broadcast_to(column[k : k + 1, :], (b, 128))
-        scale = jnp.where(row_index == k, pivot, scale)
-        work = jnp.where(row_index > k, work - (column / pivot) * row, work)
-    work = work * lax.rsqrt(scale)
-    return work[:, b : 2 * b]
+    tiles = [work[8 * t : 8 * t + 8, :] for t in range(b // 8)]
+    row_index = lax.broadcasted_iota(jnp.int32, (8, 128), 0)
+    finished = []
+    for group in range(b // 8):
+        head, below = tiles[0], tiles[1:]
+        first = 8 * group
+        wide = [
+            [jnp.broadcast_to(tile[:, first + m : first + m + 1], (8, 128)) for m in range(8)]
+            for tile in tiles
+        ]
+        entry = {
+            (i, j): jnp.broadcast_to(wide[0][j][i : i + 1, :], (8, 128))
+            for i in range(8)
+            for j in range(i + 1)
+        }
+        rows = [jnp.broadcast_to(head[i : i + 1, :], (8, 128)) for i in range(8)]
+        pivots = jnp.ones((8, 128), jnp.float32)
+        for m in range(8):
+            pivot = entry[m, m]
+            over = 1.0 / pivot
+            for i in range(m + 1, 8):
+                factor = entry[i, m] * over
+                for j in range(m + 1, i + 1):
+                    entry[i, j] = entry[i, j] - factor * entry[j, m]
+                rows[i] = rows[i] - factor * rows[m]
+                for columns in wide[1:]:
+                    columns[i] = columns[i] - factor * columns[m]
+            for t in range(len(below)):
+                below[t] = below[t] - (wide[t + 1][m] * over) * rows[m]
+            pivots = jnp.where(row_index == m, pivot, pivots)
+        merged = rows[0]
+        for m in range(1, 8):
+            merged = jnp.where(row_index == m, rows[m], merged)
+        finished.append(merged * lax.rsqrt(pivots))
+        tiles = below
+    return jnp.concatenate(finished, axis=0)[:, b : 2 * b]
 
 
 def factor_inverse(x_ref):
@@ -67,8 +95,8 @@
 
 
 def first_pass_kernel(
-    dims, maps_ref, test_ref, basis_ref, gram_ref, proj_ref,
-    part, landed, sketch, columns, factor,
+    dims, maps_hbm, test_hbm, basis_ref, gram_ref, proj_ref,
+    maps_ref, test_ref, load, part, landed, sketch, columns, factor,
     col_send, col_recv, z_send, z_recv, xy_send, xy_recv, core_send, core_recv, a_send, a_recv,
 ):
     n_row, n_col, n_z = dims
@@ -81,6 +109,21 @@
     def device(z_to, x_to, y_to, core_to):
         return (z_to * 2 + x_to, y_to * 2 + core_to)
 
+    pieces = load.shape[0]
+    depth = maps_ref.shape[-1]
+    step = depth // pieces
+    loads = []
+    for k in range(pieces):
+        span = pl.ds(k * step, step)
+        loads.append((
+            pltpu.make_async_copy(
+                maps_hbm.at[:, :, :, span], maps_ref.at[:, :, :, span], load.at[k, 0]
+            ),
+            pltpu.make_async_copy(test_hbm.at[span], test_ref.at[span], load.at[k, 1]),
+        ))
+        for copy in loads[-1]:
+            copy.start()
+
     barrier = pltpu.get_barrier_semaphore()
     for k in range(1, n_row):
         pl.semaphore_signal(
@@ -92,9 +135,14 @@
         )
 
     sub = part.shape[1]
-    depth = maps_ref.shape[-1]
-    own_maps = maps_ref[...].reshape(n_col * sub, depth)
-    part[...] = dot(own_maps, test_ref[...], (1, 0)).reshape(part.shape)
+    partial = None
+    for k in range(pieces):
+        for copy in loads[k]:
+            copy.wait()
+        span = pl.ds(k * step, step)
+        term = dot(maps_ref[:, :, :, span].reshape(n_col * sub, step), test_ref[span], (1, 0))
+        partial = term if partial is None else partial + term
+    part[...] = partial.reshape(part.shape)
     pl.semaphore_wait(barrier, n_row - 1 + n_col - 1)
 
     def send(source, target, send_sem, recv_sem, to):
@@ -264,9 +312,12 @@
             jax.ShapeDtypeStruct((size, size), f32),
             jax.ShapeDtypeStruct((size, width), f32),
         ),
-        in_specs=[VMEM, VMEM],
+        in_specs=[pl.BlockSpec(memory_space=pl.ANY)] * 2,
         out_specs=(VMEM, VMEM, VMEM),
         scratch_shapes=[
+            pltpu.VMEM(maps.shape, f32),
+            pltpu.VMEM(test_matrix.shape, f32),
+            dma((PIECES, 2)),
             pltpu.VMEM((n_col, sub, size), f32),
             pltpu.VMEM((n_col - 1, sub, size), f32),
             pltpu.VMEM((n_col // 2, 2, 2, n_z, sub, size), f32),
@@ -279,7 +330,7 @@
             dma((n_row - 1,)), dma((n_row - 1,)),
         ],
         compiler_params=pltpu.CompilerParams(
-            collective_id=0, has_side_effects=True, vmem_limit_bytes=40 * 2**20
+            collective_id=0, has_side_effects=True, vmem_limit_bytes=56 * 2**20
         ),
     )(maps, test_matrix)
     scaled, full = pl.pallas_call(
@@ -336,6 +387,7 @@
         and depth % (n_row * 128) == 0
         and size % (n_row * 8) == 0
         and size % 128 == 0
+        and depth % (PIECES * 128) == 0
         and rows * n_row * size * 4 <= 4 * 2**20
         and depth * rows * 4 <= 4 * 2**20
         and depth * size * 4 <= 4 * 2**20

time: 82.4 us -> 64.8 us (0.79); the launches traced: 81.2 us -> 64.6 us
  Pallas kernels: 77 us -> 60.4 us
    pallas_call x1, Pallas kernels: 66 us -> 41.6 us  [gathered(): pl.pallas_call(functools.partial(first_pass_kernel, (n_row, n_col, n_z)),...]
    pallas_call x1, Pallas kernels: 8.27 us -> 15.9 us  [gathered(): pl.pallas_call(functools.partial(spread_kernel, n_row), out_shape=jax.Sha...]
    unnamed x5 -> x7, local copies, waits for them, and re-layouts: 3.51 us -> 3.5 us
where the time goes in v2:
time: 64.8 us; the launch traced here: 64.6 us
  Pallas kernels  60.4 us (93%)
  local copies, waits for them, and re-layouts  3.5 us (5%)
  between operations  0.66 us (1%)
    pallas_call x1, Pallas kernels, gathered(): pl.pallas_call(functools.partial(first_pass_kernel, (n_row, n_col, n_z)),...  41.6 us
    pallas_call x1, Pallas kernels, gathered(): pl.pallas_call(functools.partial(spread_kernel, n_row), out_shape=jax.Sha...  15.9 us
    unnamed x7, local copies, waits for them, and re-layouts  3.5 us
    pallas_call x1, Pallas kernels, gathered(): pl.pallas_call(functools.partial(second_pass_kernel, rows * n_row), out_s...  2.94 us

profile of v2, /device:TPU:0, one launch (start us, length us, event | category | flops | bytes accessed | tf_op | source)
XLA Modules:
  0.0 64.6 jit_solution(8911056531358318549)
XLA Ops:
  0.6 41.6 %shard_map.41 = (f32[2,2,32,256]{3,2,1,0:T(8,128)}, f32[256,256]{1,0:T(8,128)}, f32[256,256]{1,0:T(8,128)}) custom-call(f32[2,2,32,2048]{3,2,1,0:T(8,128)} %bitcast.5, f32[2048,256]{1,0:T(8,128)} %test_hbm.1), custom_call_target="tpu_custom_call" | custom-call | tf_op jit(solution)/shard_map/pallas_call | solution.py:308
  42.3 0.0 copy-start
  42.3 0.9 %copy-done = f32[256,256]{1,0:T(8,128)S(1)} copy-done((f32[256,256]{1,0:T(8,128)S(1)}, f32[256,256]{1,0:T(8,128)}, u32[]{:S(2)}) %copy-start) | copy-done | bytes 262168
  43.2 0.0 copy-start.1
  43.2 0.9 %copy-done.1 = f32[256,256]{1,0:T(8,128)S(1)} copy-done((f32[256,256]{1,0:T(8,128)S(1)}, f32[256,256]{1,0:T(8,128)}, u32[]{:S(2)}) %copy-start.1) | copy-done | bytes 262168
  44.2 0.0 copy-start.2
  44.2 0.9 %copy-done.2 = f32[2,2,32,256]{3,2,1,0:T(8,128)S(1)} copy-done((f32[2,2,32,256]{3,2,1,0:T(8,128)S(1)}, f32[2,2,32,256]{3,2,1,0:T(8,128)}, u32[]{:S(2)}) %copy-start.2) | copy-done | bytes 131096
  45.1 2.9 %shard_map.42 = (f32[128,256]{1,0:T(8,128)}, f32[256,256]{1,0:T(8,128)S(1)}) custom-call(f32[256,256]{1,0:T(8,128)S(1)} %copy-done, f32[128,256]{1,0:T(8,128)S(1)} %bitcast.4, f32[256,256]{1,0:T(8,128)S(1)} %copy-done.1), custom_call_target="tpu_custom_call" | custom-call | tf_op jit(solution)/shard_map/pallas_call | solution.py:336
  48.0 15.9 %shard_map.43 = f32[32,2048]{1,0:T(8,128)S(1)} custom-call(f32[8,32,256]{2,1,0:T(8,128)S(1)} %bitcast.3), custom_call_target="tpu_custom_call" | custom-call | tf_op jit(solution)/shard_map/pallas_call | solution.py:347
  63.9 0.7 %copy.5 = f32[32,2048]{1,0:T(8,128)} copy(f32[32,2048]{1,0:T(8,128)S(1)} %shard_map.43) | data formatting | bytes 524288
Async XLA Ops:
  42.3 1.0 %copy-start = (f32[256,256]{1,0:T(8,128)S(1)}, f32[256,256]{1,0:T(8,128)}, u32[]{:S(2)}) copy-start(f32[256,256]{1,0:T(8,128)} %get-tuple-element.7.gram_ref) | copy-start | bytes 786436
  43.2 0.9 %copy-start.1 = (f32[256,256]{1,0:T(8,128)S(1)}, f32[256,256]{1,0:T(8,128)}, u32[]{:S(2)}) copy-start(f32[256,256]{1,0:T(8,128)} %get-tuple-element.9.proj_ref) | copy-start | bytes 786436
  44.2 0.9 %copy-start.2 = (f32[2,2,32,256]{3,2,1,0:T(8,128)S(1)}, f32[2,2,32,256]{3,2,1,0:T(8,128)}, u32[]{:S(2)}) copy-start(f32[2,2,32,256]{3,2,1,0:T(8,128)} %get-tuple-element.8) | copy-start | bytes 393220

commit v3 on v2

--- a/solution.py
+++ b/solution.py
@@ -12,15 +12,16 @@
 VMEM = pl.BlockSpec(memory_space=pltpu.VMEM)
 BLOCK = 64
 PIECES = 4
-
-
-def dot(left, right, contract):
+THREE = lax.Precision.HIGH
+
+
+def dot(left, right, contract, precision=lax.Precision.HIGHEST):
     return lax.dot_general(
         left,
         right,
         ((contract[:1], contract[1:]), ((), ())),
         preferred_element_type=jnp.float32,
-        precision=lax.Precision.HIGHEST,
+        precision=precision,
     )
 
 
@@ -134,25 +135,42 @@
             barrier, inc=1, device_id=(r, lax.rem(c + k, n_col)), device_id_type=MESH
         )
 
+    def send(source, target, send_sem, recv_sem, to):
+        copy = pltpu.make_async_remote_copy(
+            src_ref=source, dst_ref=target, send_sem=send_sem, recv_sem=recv_sem,
+            device_id=to, device_id_type=MESH,
+        )
+        copy.start()
+        return copy
+
+    a_copies = []
+
+    def exchange(steps_z, step_x):
+        for step_z in steps_z:
+            z_to, x_to = lax.rem(z + step_z, n_z), (1 - x if step_x else x)
+            to = z_to * 2 + x_to
+            span = pl.ds(pl.multiple_of(to * width, width), width)
+            k = step_z * 2 + step_x - 1
+            a_copies.append(
+                send(
+                    maps_ref.at[:, :, :, span], columns.at[:, :, x, z],
+                    a_send.at[k], a_recv.at[k], (to, c),
+                )
+            )
+
     sub = part.shape[1]
     partial = None
+    for copy, _ in loads:
+        copy.wait()
     for k in range(pieces):
-        for copy in loads[k]:
-            copy.wait()
+        if k == pieces // 2:
+            pl.semaphore_wait(barrier, n_row - 1 + n_col - 1)
+            exchange([n_z // 2], 0)
+        loads[k][1].wait()
         span = pl.ds(k * step, step)
         term = dot(maps_ref[:, :, :, span].reshape(n_col * sub, step), test_ref[span], (1, 0))
         partial = term if partial is None else partial + term
     part[...] = partial.reshape(part.shape)
-    pl.semaphore_wait(barrier, n_row - 1 + n_col - 1)
-
-    def send(source, target, send_sem, recv_sem, to):
-        copy = pltpu.make_async_remote_copy(
-            src_ref=source, dst_ref=target, send_sem=send_sem, recv_sem=recv_sem,
-            device_id=to, device_id_type=MESH,
-        )
-        copy.start()
-        return copy
-
     copies = []
     for k in range(1, n_col):
         to = lax.rem(c + k, n_col)
@@ -174,6 +192,7 @@
     for copy in copies:
         copy.wait_recv()
     sent += copies
+    exchange([k for k in range(1, n_z) if k != n_z // 2], 0)
 
     x_peer, y_peer = device(z, 1 - x, y, core), device(z, x, 1 - y, core)
     half = n_z // 2
@@ -199,28 +218,23 @@
 
     mine = sketch.at[:, core]
     core_copy = send(mine, mine, core_send, core_recv, device(z, x, y, 1 - core))
-    core_copy.wait_recv()
     sent.append(core_copy)
-
-    a_copies = []
-    for k in range(1, n_row):
-        to = lax.rem(r + k, n_row)
-        share = pl.ds(pl.multiple_of(to * width, width), width)
-        a_copies.append(
-            send(
-                maps_ref.at[:, :, :, share], columns.at[:, :, x, z],
-                a_send.at[k - 1], a_recv.at[k - 1], (to, c),
-            )
-        )
+    exchange(range(n_z), 1)
     share = pl.ds(pl.multiple_of(r * width, width), width)
     columns[:, :, x, z] = maps_ref[:, :, :, share]
 
+    def half_gram(which):
+        half_sum = None
+        for i in range(n_col // 2):
+            rows = sketch[i, which].reshape(-1, size)
+            term = dot(rows, rows, (0, 0))
+            half_sum = term if half_sum is None else half_sum + term
+        return half_sum
+
+    gram = half_gram(core)
+    core_copy.wait_recv()
+    gram = gram + half_gram(1 - core)
     chunks = [(i, j) for i in range(n_col // 2) for j in range(2)]
-    gram = None
-    for i, j in chunks:
-        rows = sketch[i, j].reshape(-1, size)
-        term = dot(rows, rows, (0, 0))
-        gram = term if gram is None else gram + term
     factor[...] = gram
     factor_inverse(factor)
     inverse = factor[...]
@@ -230,7 +244,7 @@
     for i, j in chunks:
         rows = dot(sketch[i, j].reshape(-1, size), inverse, (1, 1))
         sketch[i, j] = rows.reshape(sketch.shape[2:])
-        term = dot(rows, rows, (0, 0))
+        term = dot(rows, rows, (0, 0), THREE)
         gram = term if gram is None else gram + term
     gram_ref[...] = gram
     basis_ref[...] = sketch[:, :, x, z]
@@ -239,7 +253,8 @@
     proj = None
     for i, j in chunks:
         term = dot(
-            sketch[i, j].reshape(-1, size), columns[i, j].reshape(-1, width), (0, 0)
+            sketch[i, j].reshape(-1, size), columns[i, j].reshape(-1, width), (0, 0),
+            THREE,
         )
         proj = term if proj is None else proj + term
     proj_ref[...] = proj
@@ -268,8 +283,8 @@
         factor_inverse(factor)
 
     inverse = factor[...]
-    scaled_ref[...] = dot(basis_ref[...], inverse, (1, 1)) * math.sqrt(total_rows)
-    out_ref[...] = dot(inverse, proj_ref[...], (1, 0))
+    scaled_ref[...] = dot(basis_ref[...], inverse, (1, 1), THREE) * math.sqrt(total_rows)
+    out_ref[...] = dot(inverse, proj_ref[...], (1, 0), THREE)
 
 
 def spread_kernel(n_row, proj_ref, out_ref, send_sem, recv_sem):
@@ -312,7 +327,7 @@
             jax.ShapeDtypeStruct((size, size), f32),
             jax.ShapeDtypeStruct((size, width), f32),
         ),
-        in_specs=[pl.BlockSpec(memory_space=pl.ANY)] * 2,
+        in_specs=[pl.BlockSpec(memory_space=pltpu.HBM)] * 2,
         out_specs=(VMEM, VMEM, VMEM),
         scratch_shapes=[
             pltpu.VMEM(maps.shape, f32),
@@ -330,7 +345,7 @@
             dma((n_row - 1,)), dma((n_row - 1,)),
         ],
         compiler_params=pltpu.CompilerParams(
-            collective_id=0, has_side_effects=True, vmem_limit_bytes=56 * 2**20
+            collective_id=0, has_side_effects=True, vmem_limit_bytes=53 * 2**20
         ),
     )(maps, test_matrix)
     scaled, full = pl.pallas_call(

time: 64.8 us -> 61.2 us (0.944)
  the two profiles are of different devices: /device:TPU:0 before, /device:TPU:15 now
where the time goes in v3:
time: 61.2 us; the launch traced here: 61.1 us
  Pallas kernels  59.7 us (98%)
  local copies, waits for them, and re-layouts  0.71 us (1%)
  between operations  0.65 us (1%)
    pallas_call x1, Pallas kernels, gathered(): pl.pallas_call(functools.partial(first_pass_kernel, (n_row, n_col, n_z)),...  42.9 us
    pallas_call x1, Pallas kernels, gathered(): pl.pallas_call(functools.partial(spread_kernel, n_row), out_shape=jax.Sha...  14.3 us
    pallas_call x1, Pallas kernels, gathered(): pl.pallas_call(functools.partial(second_pass_kernel, rows * n_row), out_s...  2.55 us

profile of v3, /device:TPU:15, one launch (start us, length us, event | category | flops | bytes accessed | tf_op | source)
XLA Modules:
  0.0 61.1 jit_solution(3890851331242182411)
XLA Ops:
  0.6 42.9 %shard_map.41 = (f32[2,2,32,256]{3,2,1,0:T(8,128)S(1)}, f32[256,256]{1,0:T(8,128)S(1)}, f32[256,256]{1,0:T(8,128)S(1)}) custom-call(f32[2,2,32,2048]{3,2,1,0:T(8,128)} %bitcast.5, f32[2048,256]{1,0:T(8,128)} %test_hbm.1), custom_call_target="tpu_custom_call" | custom-call | tf_op jit(solution)/shard_map/pallas_call | solution.py:323
  43.5 2.5 %shard_map.42 = (f32[128,256]{1,0:T(8,128)}, f32[256,256]{1,0:T(8,128)S(1)}) custom-call(f32[256,256]{1,0:T(8,128)S(1)} %get-tuple-element.7.gram_ref, f32[128,256]{1,0:T(8,128)S(1)} %bitcast.4, f32[256,256]{1,0:T(8,128)S(1)} %get-tuple-element.9.proj_ref), custom_call_target="tpu_custom_call" | custom-call | tf_op jit(solution)/shard_map/pallas_call | solution.py:351
  46.0 14.3 %shard_map.43 = f32[32,2048]{1,0:T(8,128)S(1)} custom-call(f32[8,32,256]{2,1,0:T(8,128)S(1)} %bitcast.3), custom_call_target="tpu_custom_call" | custom-call | tf_op jit(solution)/shard_map/pallas_call | solution.py:362
  60.4 0.7 %copy.5 = f32[32,2048]{1,0:T(8,128)} copy(f32[32,2048]{1,0:T(8,128)S(1)} %shard_map.43) | data formatting | bytes 524288

commit v4 on v3

--- a/solution.py
+++ b/solution.py
@@ -99,6 +99,7 @@
     dims, maps_hbm, test_hbm, basis_ref, gram_ref, proj_ref,
     maps_ref, test_ref, load, part, landed, sketch, columns, factor,
     col_send, col_recv, z_send, z_recv, xy_send, xy_recv, core_send, core_recv, a_send, a_recv,
+    relay, x_send, x_recv,
 ):
     n_row, n_col, n_z = dims
     r, c = lax.axis_index("row"), lax.axis_index("col")
@@ -143,21 +144,38 @@
         copy.start()
         return copy
 
-    a_copies = []
-
-    def exchange(steps_z, step_x):
-        for step_z in steps_z:
-            z_to, x_to = lax.rem(z + step_z, n_z), (1 - x if step_x else x)
-            to = z_to * 2 + x_to
-            span = pl.ds(pl.multiple_of(to * width, width), width)
-            k = step_z * 2 + step_x - 1
-            a_copies.append(
+    def share(z_to, x_to):
+        start = pl.multiple_of((z_to * 2 + x_to) * width, width)
+        return maps_ref.at[:, :, :, pl.ds(start, width)]
+
+    x_peer, y_peer = device(z, 1 - x, y, core), device(z, x, 1 - y, core)
+    x_copies, z_copies = [], []
+
+    def exchange_x():
+        for d in list(range(1, n_z)) + [0]:
+            target = relay.at[d - 1] if d else columns.at[:, :, x, z]
+            x_copies.append(
                 send(
-                    maps_ref.at[:, :, :, span], columns.at[:, :, x, z],
-                    a_send.at[k], a_recv.at[k], (to, c),
+                    share(lax.rem(z + d, n_z), 1 - x), target,
+                    x_send.at[d], x_recv.at[d], x_peer,
                 )
             )
 
+    def exchange_z(distances, passed_on):
+        for d in distances:
+            z_to = lax.rem(z + d, n_z)
+            source = relay.at[d - 1] if passed_on else share(z_to, x)
+            k = d - 1 + (n_z - 1 if passed_on else 0)
+            from_x = 1 - x if passed_on else x
+            z_copies.append(
+                send(
+                    source, columns.at[:, :, from_x, z],
+                    a_send.at[k], a_recv.at[k], device(z_to, x, y, core),
+                )
+            )
+
+    far = n_z // 2
+    others = [d for d in range(1, n_z) if d != far]
     sub = part.shape[1]
     partial = None
     for copy, _ in loads:
@@ -165,7 +183,8 @@
     for k in range(pieces):
         if k == pieces // 2:
             pl.semaphore_wait(barrier, n_row - 1 + n_col - 1)
-            exchange([n_z // 2], 0)
+            exchange_z([far], False)
+            exchange_x()
         loads[k][1].wait()
         span = pl.ds(k * step, step)
         term = dot(maps_ref[:, :, :, span].reshape(n_col * sub, step), test_ref[span], (1, 0))
@@ -192,9 +211,7 @@
     for copy in copies:
         copy.wait_recv()
     sent += copies
-    exchange([k for k in range(1, n_z) if k != n_z // 2], 0)
-
-    x_peer, y_peer = device(z, 1 - x, y, core), device(z, x, 1 - y, core)
+
     half = n_z // 2
     low, high = pl.ds(0, half), pl.ds(half, half)
     a = sketch.at[y, core, x, low]
@@ -203,6 +220,7 @@
         send(a, a, xy_send.at[0], xy_recv.at[0], x_peer),
         send(b, b, xy_send.at[1], xy_recv.at[1], y_peer),
     ]
+    exchange_z(others, False)
     for copy in copies:
         copy.wait_recv()
     sent += copies
@@ -212,6 +230,9 @@
         send(a, a, xy_send.at[2], xy_recv.at[2], y_peer),
         send(b, b, xy_send.at[3], xy_recv.at[3], x_peer),
     ]
+    for d in [far] + others:
+        x_copies[d - 1].wait_recv()
+        exchange_z([d], True)
     for copy in copies:
         copy.wait_recv()
     sent += copies
@@ -219,9 +240,7 @@
     mine = sketch.at[:, core]
     core_copy = send(mine, mine, core_send, core_recv, device(z, x, y, 1 - core))
     sent.append(core_copy)
-    exchange(range(n_z), 1)
-    share = pl.ds(pl.multiple_of(r * width, width), width)
-    columns[:, :, x, z] = maps_ref[:, :, :, share]
+    columns[:, :, x, z] = share(z, x)[...]
 
     def half_gram(which):
         half_sum = None
@@ -238,7 +257,7 @@
     factor[...] = gram
     factor_inverse(factor)
     inverse = factor[...]
-    for copy in sent:
+    for copy in sent + x_copies:
         copy.wait_send()
     gram = None
     for i, j in chunks:
@@ -248,7 +267,8 @@
         gram = term if gram is None else gram + term
     gram_ref[...] = gram
     basis_ref[...] = sketch[:, :, x, z]
-    for copy in a_copies:
+    x_copies[-1].wait_recv()
+    for copy in z_copies:
         copy.wait()
     proj = None
     for i, j in chunks:
@@ -342,7 +362,9 @@
             dma((n_z - 1,)), dma((n_z - 1,)),
             dma((4,)), dma((4,)),
             dma, dma,
-            dma((n_row - 1,)), dma((n_row - 1,)),
+            dma((2 * n_z - 2,)), dma((2 * n_z - 2,)),
+            pltpu.VMEM((n_z - 1, n_col // 2, 2, sub, width), f32),
+            dma((n_z,)), dma((n_z,)),
         ],
         compiler_params=pltpu.CompilerParams(
             collective_id=0, has_side_effects=True, vmem_limit_bytes=53 * 2**20

time: 61.2 us -> 53.9 us (0.88)
  the two profiles are of different devices: /device:TPU:15 before, /device:TPU:0 now
where the time goes in v4:
time: 53.9 us; the launch traced here: 53.7 us
  Pallas kernels  52.4 us (97%)
  local copies, waits for them, and re-layouts  0.71 us (1%)
  between operations  0.65 us (1%)
    pallas_call x1, Pallas kernels, gathered(): pl.pallas_call(functools.partial(first_pass_kernel, (n_row, n_col, n_z)),...  40.4 us
    pallas_call x1, Pallas kernels, gathered(): pl.pallas_call(functools.partial(spread_kernel, n_row), out_shape=jax.Sha...  9.48 us
    pallas_call x1, Pallas kernels, gathered(): pl.pallas_call(functools.partial(second_pass_kernel, rows * n_row), out_s...  2.55 us

profile of v4, /device:TPU:0, one launch (start us, length us, event | category | flops | bytes accessed | tf_op | source)
XLA Modules:
  0.0 53.7 jit_solution(8863823952439198803)
XLA Ops:
  0.6 40.4 %shard_map.41 = (f32[2,2,32,256]{3,2,1,0:T(8,128)S(1)}, f32[256,256]{1,0:T(8,128)S(1)}, f32[256,256]{1,0:T(8,128)S(1)}) custom-call(f32[2,2,32,2048]{3,2,1,0:T(8,128)} %bitcast.5, f32[2048,256]{1,0:T(8,128)} %test_hbm.1), custom_call_target="tpu_custom_call" | custom-call | tf_op jit(solution)/shard_map/pallas_call | solution.py:343
  41.0 2.5 %shard_map.42 = (f32[128,256]{1,0:T(8,128)}, f32[256,256]{1,0:T(8,128)S(1)}) custom-call(f32[256,256]{1,0:T(8,128)S(1)} %get-tuple-element.7.gram_ref, f32[128,256]{1,0:T(8,128)S(1)} %bitcast.4, f32[256,256]{1,0:T(8,128)S(1)} %get-tuple-element.9.proj_ref), custom_call_target="tpu_custom_call" | custom-call | tf_op jit(solution)/shard_map/pallas_call | solution.py:373
  43.6 9.5 %shard_map.43 = f32[32,2048]{1,0:T(8,128)S(1)} custom-call(f32[8,32,256]{2,1,0:T(8,128)S(1)} %bitcast.3), custom_call_target="tpu_custom_call" | custom-call | tf_op jit(solution)/shard_map/pallas_call | solution.py:384
  53.0 0.7 %copy.5 = f32[32,2048]{1,0:T(8,128)} copy(f32[32,2048]{1,0:T(8,128)S(1)} %shard_map.43) | data formatting | bytes 524288

commit v5 on v4

--- a/solution.py
+++ b/solution.py
@@ -72,27 +72,23 @@
     size = x_ref.shape[0]
     lane = lax.broadcasted_iota(jnp.int32, (BLOCK, size), 1)
     row_index = lax.broadcasted_iota(jnp.int32, (BLOCK, size), 0)
-    all_rows = lax.broadcasted_iota(jnp.int32, (size, size), 0)
-    all_lanes = lax.broadcasted_iota(jnp.int32, (size, size), 1)
-
-    def step(i, carry):
-        start = pl.multiple_of(i * BLOCK, BLOCK)
-        rows = x_ref[pl.ds(start, BLOCK), :]
-        diagonal = pltpu.roll(rows, lax.rem(size - start, size), 1)[:, :128]
+    for start in range(0, size, BLOCK):
+        end = start + BLOCK
+        rows = x_ref[start:end, :]
+        diagonal = (pltpu.roll(rows, size - start, 1) if start else rows)[:, :128]
         inverse = small_inverse(diagonal)
-        inside = (lane >= start) & (lane < start + BLOCK)
+        inside = (lane >= start) & (lane < end)
         rows = jnp.where(inside, jnp.where(lane == start + row_index, 1.0, 0.0), rows)
         done = dot(inverse, rows, (1, 0))
-        upper = jnp.where(lane >= start + BLOCK, done, 0.0)
-        update = dot(upper, done, (0, 0))
-        below = all_rows >= start + BLOCK
-        cleared = (all_lanes >= start) & (all_lanes < start + BLOCK)
-        x_ref[...] = jnp.where(below & cleared, 0.0, x_ref[...]) - update
-        x_ref[pl.ds(start, BLOCK), :] = done
-        return carry
-
-    lax.fori_loop(0, size // BLOCK, step, 0)
-    x_ref[...] = jnp.where(all_lanes <= all_rows, x_ref[...], 0.0)
+        if end < size:
+            low = end // 128 * 128
+            upper = jnp.where(lane >= end, done, 0.0)[:, low:]
+            update = dot(upper, done, (0, 0))
+            rest_rows = low + lax.broadcasted_iota(jnp.int32, update.shape, 0)
+            rest_lanes = lax.broadcasted_iota(jnp.int32, update.shape, 1)
+            cleared = (rest_rows >= end) & (rest_lanes >= start) & (rest_lanes < end)
+            x_ref[low:, :] = jnp.where(cleared, 0.0, x_ref[low:, :]) - update
+        x_ref[start:end, :] = jnp.where(lane <= start + row_index, done, 0.0)
 
 
 def first_pass_kernel(
@@ -259,25 +255,19 @@
     inverse = factor[...]
     for copy in sent + x_copies:
         copy.wait_send()
-    gram = None
+    x_copies[-1].wait_recv()
+    for copy in z_copies:
+        copy.wait()
+    both = None
     for i, j in chunks:
         rows = dot(sketch[i, j].reshape(-1, size), inverse, (1, 1))
         sketch[i, j] = rows.reshape(sketch.shape[2:])
-        term = dot(rows, rows, (0, 0), THREE)
-        gram = term if gram is None else gram + term
-    gram_ref[...] = gram
+        wide = jnp.concatenate([rows, columns[i, j].reshape(-1, width)], axis=1)
+        term = dot(rows, wide, (0, 0), THREE)
+        both = term if both is None else both + term
+    gram_ref[...] = both[:, :size]
+    proj_ref[...] = both[:, size:]
     basis_ref[...] = sketch[:, :, x, z]
-    x_copies[-1].wait_recv()
-    for copy in z_copies:
-        copy.wait()
-    proj = None
-    for i, j in chunks:
-        term = dot(
-            sketch[i, j].reshape(-1, size), columns[i, j].reshape(-1, width), (0, 0),
-            THREE,
-        )
-        proj = term if proj is None else proj + term
-    proj_ref[...] = proj
 
 
 def second_pass_kernel(total_rows, gram_ref, basis_ref, proj_ref, scaled_ref, out_ref, factor):
@@ -319,7 +309,7 @@
     out_ref[:, share] = proj_ref[r]
     pl.semaphore_wait(barrier, n_row - 1)
     copies = []
-    for k in range(1, n_row):
+    for k in sorted(range(1, n_row), key=lambda step: abs(step - n_row // 2)):
         to = lax.rem(r + k, n_row)
         copy = pltpu.make_async_remote_copy(
             src_ref=proj_ref.at[to], dst_ref=out_ref.at[:, share],

time: 53.9 us -> 54 us (level)
    pallas_call x1, Pallas kernels: 9.48 us -> 10.7 us  [gathered(): pl.pallas_call(functools.partial(spread_kernel, n_row), out_shape=jax.Sha...]
    pallas_call x1, Pallas kernels: 40.4 us -> 39.3 us  [gathered(): pl.pallas_call(functools.partial(first_pass_kernel, (n_row, n_col, n_z)),...]
where the time goes in v5:
time: 54 us; the launch traced here: 53.9 us
  Pallas kernels  52.5 us (97%)
  local copies, waits for them, and re-layouts  0.71 us (1%)
  between operations  0.65 us (1%)
    pallas_call x1, Pallas kernels, gathered(): pl.pallas_call(functools.partial(first_pass_kernel, (n_row, n_col, n_z)),...  39.3 us
    pallas_call x1, Pallas kernels, gathered(): pl.pallas_call(functools.partial(spread_kernel, n_row), out_shape=jax.Sha...  10.7 us
    pallas_call x1, Pallas kernels, gathered(): pl.pallas_call(functools.partial(second_pass_kernel, rows * n_row), out_s...  2.56 us

profile of v5, /device:TPU:0, one launch (start us, length us, event | category | flops | bytes accessed | tf_op | source)
XLA Modules:
  0.0 53.9 jit_solution(3286510439167144145)
XLA Ops:
  0.6 39.3 %shard_map.41 = (f32[2,2,32,256]{3,2,1,0:T(8,128)S(1)}, f32[256,256]{1,0:T(8,128)S(1)}, f32[256,256]{1,0:T(8,128)S(1)}) custom-call(f32[2,2,32,2048]{3,2,1,0:T(8,128)} %bitcast.5, f32[2048,256]{1,0:T(8,128)} %test_hbm.1), custom_call_target="tpu_custom_call" | custom-call | tf_op jit(solution)/shard_map/pallas_call | solution.py:333
  39.9 2.6 %shard_map.42 = (f32[128,256]{1,0:T(8,128)}, f32[256,256]{1,0:T(8,128)S(1)}) custom-call(f32[256,256]{1,0:T(8,128)S(1)} %get-tuple-element.7.gram_ref, f32[128,256]{1,0:T(8,128)S(1)} %bitcast.4, f32[256,256]{1,0:T(8,128)S(1)} %get-tuple-element.9.proj_ref), custom_call_target="tpu_custom_call" | custom-call | tf_op jit(solution)/shard_map/pallas_call | solution.py:363
  42.5 10.7 %shard_map.43 = f32[32,2048]{1,0:T(8,128)S(1)} custom-call(f32[8,32,256]{2,1,0:T(8,128)S(1)} %bitcast.3), custom_call_target="tpu_custom_call" | custom-call | tf_op jit(solution)/shard_map/pallas_call | solution.py:374
  53.2 0.7 %copy.5 = f32[32,2048]{1,0:T(8,128)} copy(f32[32,2048]{1,0:T(8,128)S(1)} %shard_map.43) | data formatting | bytes 524288

commit v6 on v4

--- a/solution.py
+++ b/solution.py
@@ -53,7 +53,7 @@
             for i in range(m + 1, 8):
                 factor = entry[i, m] * over
                 for j in range(m + 1, i + 1):
-                    entry[i, j] = entry[i, j] - factor * entry[j, m]
+                    entry[i, j] = entry[i, j] - (entry[i, m] * entry[j, m]) * over
                 rows[i] = rows[i] - factor * rows[m]
                 for columns in wide[1:]:
                     columns[i] = columns[i] - factor * columns[m]
@@ -259,25 +259,19 @@
     inverse = factor[...]
     for copy in sent + x_copies:
         copy.wait_send()
-    gram = None
+    x_copies[-1].wait_recv()
+    for copy in z_copies:
+        copy.wait()
+    both = None
     for i, j in chunks:
         rows = dot(sketch[i, j].reshape(-1, size), inverse, (1, 1))
         sketch[i, j] = rows.reshape(sketch.shape[2:])
-        term = dot(rows, rows, (0, 0), THREE)
-        gram = term if gram is None else gram + term
-    gram_ref[...] = gram
+        wide = jnp.concatenate([rows, columns[i, j].reshape(-1, width)], axis=1)
+        term = dot(rows, wide, (0, 0), THREE)
+        both = term if both is None else both + term
+    gram_ref[...] = both[:, :size]
+    proj_ref[...] = both[:, size:]
     basis_ref[...] = sketch[:, :, x, z]
-    x_copies[-1].wait_recv()
-    for copy in z_copies:
-        copy.wait()
-    proj = None
-    for i, j in chunks:
-        term = dot(
-            sketch[i, j].reshape(-1, size), columns[i, j].reshape(-1, width), (0, 0),
-            THREE,
-        )
-        proj = term if proj is None else proj + term
-    proj_ref[...] = proj
 
 
 def second_pass_kernel(total_rows, gram_ref, basis_ref, proj_ref, scaled_ref, out_ref, factor):

time: 53.9 us -> 53.7 us (level)
  no operation moved by 1% of the time
where the time goes in v6:
time: 53.7 us; the launch traced here: 53.6 us
  Pallas kernels  52.2 us (97%)
  local copies, waits for them, and re-layouts  0.71 us (1%)
  between operations  0.65 us (1%)
    pallas_call x1, Pallas kernels, gathered(): pl.pallas_call(functools.partial(first_pass_kernel, (n_row, n_col, n_z)),...  40.2 us
    pallas_call x1, Pallas kernels, gathered(): pl.pallas_call(functools.partial(spread_kernel, n_row), out_shape=jax.Sha...  9.49 us
    pallas_call x1, Pallas kernels, gathered(): pl.pallas_call(functools.partial(second_pass_kernel, rows * n_row), out_s...  2.55 us

profile of v6, /device:TPU:0, one launch (start us, length us, event | category | flops | bytes accessed | tf_op | source)
XLA Modules:
  0.0 53.6 jit_solution(13056605025545102891)
XLA Ops:
  0.6 40.2 %shard_map.41 = (f32[2,2,32,256]{3,2,1,0:T(8,128)S(1)}, f32[256,256]{1,0:T(8,128)S(1)}, f32[256,256]{1,0:T(8,128)S(1)}) custom-call(f32[2,2,32,2048]{3,2,1,0:T(8,128)} %bitcast.5, f32[2048,256]{1,0:T(8,128)} %test_hbm.1), custom_call_target="tpu_custom_call" | custom-call | tf_op jit(solution)/shard_map/pallas_call | solution.py:337
  40.8 2.5 %shard_map.42 = (f32[128,256]{1,0:T(8,128)}, f32[256,256]{1,0:T(8,128)S(1)}) custom-call(f32[256,256]{1,0:T(8,128)S(1)} %get-tuple-element.7.gram_ref, f32[128,256]{1,0:T(8,128)S(1)} %bitcast.4, f32[256,256]{1,0:T(8,128)S(1)} %get-tuple-element.9.proj_ref), custom_call_target="tpu_custom_call" | custom-call | tf_op jit(solution)/shard_map/pallas_call | solution.py:367
  43.4 9.5 %shard_map.43 = f32[32,2048]{1,0:T(8,128)S(1)} custom-call(f32[8,32,256]{2,1,0:T(8,128)S(1)} %bitcast.3), custom_call_target="tpu_custom_call" | custom-call | tf_op jit(solution)/shard_map/pallas_call | solution.py:378
  52.9 0.7 %copy.5 = f32[32,2048]{1,0:T(8,128)} copy(f32[32,2048]{1,0:T(8,128)S(1)} %shard_map.43) | data formatting | bytes 524288
